TPU v7x, 1024 devices: a whole 8x8x8 slice. The times are simulated.
1024 devices in a mesh: curve: 128 (over x, y, core), level: 8 (over z).
Axes of the slice: x: 8, y: 8, z: 8, core: 2. Of those that a mesh axis runs over, the one named last changes fastest.
Arguments:
- coarse_pops: float32 [19, 128, 64, 128], P(None, 'curve', 'level'), may hold values from 0.33 to 9.34, as said below
- medium_pops: float32 [19, 256, 64, 256], P(None, 'curve', 'level'), may hold values from 0.33 to 9.34, as said below
- fine_pops: float32 [19, 512, 64, 512], P(None, 'curve', 'level'), may hold values from 0.33 to 9.34, as said below
- solid_cells: int32 [512, 64, 512], P('curve', 'level'), may hold values from 0 to 1, as said below
- shear_rate: float32 [128, 8], P('curve', 'level'), may hold values from 0.7 to 1.9
Outputs:
- advanced_coarse: float32 [19, 128, 64, 128], P(None, 'curve', 'level')
- advanced_medium: float32 [19, 256, 64, 256], P(None, 'curve', 'level')
- advanced_fine: float32 [19, 512, 64, 512], P(None, 'curve', 'level')
Inputs may be any that keep to these rules, and one draw needn't show every extreme that they name: `coarse_pops`: every population is 20 times its lattice weight w_q times a factor between 0.6 and 1.4. `medium_pops`: every population is 20 times its lattice weight w_q times a factor between 0.6 and 1.4. `fine_pops`: every population is 20 times its lattice weight w_q times a factor between 0.6 and 1.4. `solid_cells`: no cell of the top two rows along the second dimension is solid; a solid cell (x, y, z) has x % 4 in 1 .. 2 and y % 8 in 1 .. 6.
All inputs are finite; a program needn't handle non-finite values.
Results may differ from a plain program's by a relative error of at most 0.0003.
Values sent between devices are 32-bit elements; how exact they have to be, the bound alone decides.
A program may use at most 128 MiB of HBM per device.

v0:
```python
import jax
import jax.numpy as jnp
from jax import lax
from jax.experimental import pallas as pl
from jax.experimental.pallas import tpu as pltpu
from jax.sharding import PartitionSpec as P

VELOCITIES = [
    (0, 0, 0),
    (1, 0, 0),
    (-1, 0, 0),
    (0, 1, 0),
    (0, -1, 0),
    (0, 0, 1),
    (0, 0, -1),
    (1, 1, 0),
    (-1, -1, 0),
    (1, -1, 0),
    (-1, 1, 0),
    (1, 0, 1),
    (-1, 0, -1),
    (1, 0, -1),
    (-1, 0, 1),
    (0, 1, 1),
    (0, -1, -1),
    (0, 1, -1),
    (0, -1, 1),
]
OPPOSITE = [0, 2, 1, 4, 3, 6, 5, 8, 7, 10, 9, 12, 11, 14, 13, 16, 15, 18, 17]

ORDER = [1, 7, 9, 11, 13, 2, 8, 10, 12, 14, 0, 3, 4, 5, 6, 15, 16, 17, 18]
PLACE = [ORDER.index(q) for q in range(19)]
UPWARD = [7, 3, 10, 15, 17]
DOWNWARD = [9, 4, 8, 16, 18]
ROWS = 8
LANES = 128
SOLID = float("nan")


def collide(f, rate, solid):
    s = {}
    d = {}
    for q in (1, 3, 5, 7, 9, 11, 13, 15, 17):
        s[q] = f[q] + f[q + 1]
        d[q] = f[q] - f[q + 1]
    xy, xz, yz = s[7] + s[9], s[11] + s[13], s[15] + s[17]
    pxy, pxz, pyz = s[7] - s[9], s[11] - s[13], s[15] - s[17]
    axis_sum = s[1] + s[3] + s[5]
    edge_sum = xy + xz + yz
    density = f[0] + axis_sum + edge_sum
    if solid is not None:
        density = jnp.where(solid, SOLID, density)
    inverse = 1.0 / density
    x_xy, y_xy = d[7] + d[9], d[7] - d[9]
    x_xz, z_xz = d[11] + d[13], d[11] - d[13]
    y_yz, z_yz = d[15] + d[17], d[15] - d[17]
    sum_x, sum_y, sum_z = x_xy + x_xz, y_xy + y_yz, z_xz + z_yz
    jx, jy, jz = d[1] + sum_x, d[3] + sum_y, d[5] + sum_z
    ux, uy, uz = jx * inverse, jy * inverse, jz * inverse
    xx, yy, zz = jx * ux, jy * uy, jz * uz
    yy_zz = yy + zz
    energy = xx + yy_zz

    tx, ty, tz = sum_x - 2.0 * d[1], sum_y - 2.0 * d[3], sum_z - 2.0 * d[5]
    mx = 0.2475 * (x_xy - x_xz)
    my = 0.2475 * (y_yz - y_xy)
    mz = 0.2475 * (z_xz - z_yz)
    hx, hy, hz = 0.05 * tx, 0.05 * ty, 0.05 * tz
    ax, ay, az = 0.2 * tx, 0.2 * ty, 0.2 * tz
    x1, x2 = hx + mx, hx - mx
    y1, y2 = hy - my, hy + my
    z1, z2 = hz + mz, hz - mz

    alpha = (1.19 * 19.0 / 2394.0) * (edge_sum - f[0] - energy)
    beta = (1.4 / 252.0) * (9.0 * f[0] - 7.0 * axis_sum - 2.0 * edge_sum + 5.5 * energy)
    base0 = 30.0 * alpha - 12.0 * beta
    base1 = 11.0 * alpha + 4.0 * beta
    base2 = 8.0 * alpha + beta
    u1 = 3.0 * s[1] - axis_sum
    u2 = edge_sum - 3.0 * yz
    pxx = 2.0 * xx - yy_zz
    gamma = (rate * (1.0 / 36.0)) * (u1 + u2 - pxx)
    delta = (1.4 / 72.0) * (u2 - 2.0 * u1 + 0.5 * pxx)
    v1 = s[3] - s[5]
    v2 = xy - xz
    ww = yy - zz
    eps = (rate * (1.0 / 12.0)) * (v1 + v2 - ww)
    zeta = (1.4 / 24.0) * (v2 - 2.0 * v1 + 0.5 * ww)
    g1, g2 = gamma - 2.0 * delta, gamma + delta
    h1, h2 = eps - 2.0 * zeta, eps + zeta
    quarter = rate * 0.25
    nxy = quarter * (pxy - jx * uy)
    nxz = quarter * (pxz - jx * uz)
    nyz = quarter * (pyz - jy * uz)
    ex = base1 - 2.0 * g1
    eyz = base1 + g1
    ey, ez = eyz - h1, eyz + h1
    low = base2 + g2
    exy, exz = low + h2, low - h2
    eyz2 = base2 - 2.0 * g2
    out = [None] * 19
    out[0] = f[0] + base0
    for q, even, odd in ((1, ex, ax), (3, ey, ay), (5, ez, az)):
        out[q] = f[q] + (even + odd)
        out[q + 1] = f[q + 1] + (even - odd)
    for q, even, odd in (
        (7, exy + nxy, x1 + y1),
        (9, exy - nxy, x1 - y1),
        (11, exz + nxz, x2 + z1),
        (13, exz - nxz, x2 - z1),
        (15, eyz2 + nyz, y2 + z2),
        (17, eyz2 - nyz, y2 - z2),
    ):
        out[q] = f[q] - (even + odd)
        out[q + 1] = f[q + 1] - (even - odd)
    return out


class Level:
    def __init__(self, width, tiles, relaxed, sent, came, send_sem, recv_sem):
        self.width, self.tiles = width, tiles
        self.relaxed, self.sent, self.came = relaxed, sent, came
        self.send_sem, self.recv_sem = send_sem, recv_sem

    def copies(self, turn, around):
        width, tiles = self.width, self.tiles
        third = (2 * tiles // ROWS) * ROWS
        relaxed, sent, came = self.relaxed, self.sent, self.came
        (left, right), (below, above), (me_x, me_y) = around

        def copy(no, source, target, device):
            return pltpu.make_async_remote_copy(
                src_ref=source,
                dst_ref=target,
                send_sem=self.send_sem.at[turn, no],
                recv_sem=self.recv_sem.at[turn, no],
                device_id=device,
                device_id_type=pl.DeviceIdType.MESH,
            )

        rows = pl.ds(1, width)
        first, last = pl.ds(0, ROWS), pl.ds(third, ROWS)
        result = [
            copy(0, relaxed.at[turn, pl.ds(0, 5), width], relaxed.at[turn, pl.ds(0, 5), 0], (right, me_y)),
            copy(1, relaxed.at[turn, pl.ds(5, 5), 1], relaxed.at[turn, pl.ds(5, 5), width + 1], (left, me_y)),
        ]
        for way, beyond in ((0, above), (1, below)):
            result.append(copy(2 + way, sent.at[turn, way, rows], came.at[turn, way, rows], (me_x, beyond)))
        for way, beyond in ((0, above), (1, below)):
            result.append(
                copy(4 + way, sent.at[turn, way, width, first], came.at[turn, way, 0, first], (right, beyond))
            )
            result.append(
                copy(6 + way, sent.at[turn, way, 1, last], came.at[turn, way, width + 1, last], (left, beyond))
            )
        return result

    def keep(self, turn, x, tile, values):
        for q in range(19):
            self.relaxed[turn, PLACE[q], x + 1, tile] = values[q]
        for way, group, row in ((0, UPWARD, ROWS - 1), (1, DOWNWARD, 0)):
            for no, q in enumerate(group):
                self.sent[turn, way, x + 1, pl.ds(no * self.tiles + tile, 1), :] = values[q][row : row + 1, :]

    def streamed(self, turn, x, tile, blocked):
        lane = lax.broadcasted_iota(jnp.int32, (ROWS, LANES), 1)
        row = lax.broadcasted_iota(jnp.int32, (ROWS, LANES), 0)
        relaxed, came, tiles = self.relaxed, self.came, self.tiles
        values = []
        for q, (step_x, step_y, step_z) in enumerate(VELOCITIES):
            plane = x + 1 - step_x
            place = PLACE[q]
            value = relaxed[turn, place, plane, tile]
            beside = (tile - step_z) % tiles
            crossing = lane == (LANES - 1 if step_z > 0 else 0)
            if step_z != 0 and tiles > 1:
                value = jnp.where(crossing, relaxed[turn, place, plane, beside], value)
            if step_y != 0:
                way = 0 if step_y > 0 else 1
                no = (UPWARD if step_y > 0 else DOWNWARD).index(q) * tiles

                def ghost(at):
                    line = came[turn, way, plane, pl.ds(no + at, 1), :]
                    return jnp.broadcast_to(line, (ROWS, LANES))

                edge = ghost(tile)
                if step_z != 0 and tiles > 1:
                    edge = jnp.where(crossing, ghost(beside), edge)
                value = pltpu.roll(value, 1 if step_y > 0 else ROWS - 1, 0)
                value = jnp.where(row == (0 if step_y > 0 else ROWS - 1), edge, value)
            if step_z != 0:
                value = pltpu.roll(value, 1 if step_z > 0 else LANES - 1, 1)
            if q in blocked:
                value = jnp.where(value != value, relaxed[turn, PLACE[OPPOSITE[q]], x + 1, tile], value)
            values.append(value)
        return values


def coalesce(fine, fine_turn, coarse, coarse_turn, pairs, halves):
    lane = lax.broadcasted_iota(jnp.int32, (ROWS, LANES), 1)
    for x in range(coarse.width):
        for no, q in enumerate(UPWARD):
            for tile in range(fine.tiles):
                both = (
                    fine.relaxed[fine_turn, PLACE[q], 2 * x + 1, tile]
                    + fine.relaxed[fine_turn, PLACE[q], 2 * x + 2, tile]
                )
                both = both + pltpu.roll(both, 1, 0)
                pairs[tile, pl.ds(5 * x + no, 1), :] = both[ROWS - 1 : ROWS, :]
    for block in range((5 * coarse.width + ROWS - 1) // ROWS):
        rows = pl.ds(block * ROWS, ROWS)
        packed = []
        for tile in range(fine.tiles):
            value = pairs[tile, rows, :]
            value = (value + pltpu.roll(value, LANES - 1, 1)) * 0.125
            for bit in range(6):
                shifted = pltpu.roll(value, LANES - 2**bit, 1)
                value = jnp.where((lane & 2**bit) != 0, shifted, value)
            packed.append(value)
        for tile in range(coarse.tiles):
            upper = pltpu.roll(packed[2 * tile + 1], LANES // 2, 1)
            halves[tile, rows, :] = jnp.where(lane < LANES // 2, packed[2 * tile], upper)
    for x in range(coarse.width):
        for no in range(5):
            for tile in range(coarse.tiles):
                coarse.sent[coarse_turn, 0, x + 1, pl.ds(no * coarse.tiles + tile, 1), :] = halves[
                    tile, pl.ds(5 * x + no, 1), :
                ]


def explode(coarse, coarse_turn, fine, fine_turn, pairs, halves):
    lane = lax.broadcasted_iota(jnp.int32, (ROWS, LANES), 1)
    for x in range(coarse.width):
        for no, q in enumerate(DOWNWARD):
            for tile in range(coarse.tiles):
                halves[tile, pl.ds(5 * x + no, 1), :] = coarse.relaxed[
                    coarse_turn, PLACE[q], x + 1, tile, pl.ds(0, 1), :
                ]
    for block in range((5 * coarse.width + ROWS - 1) // ROWS):
        rows = pl.ds(block * ROWS, ROWS)
        for tile in range(fine.tiles):
            value = halves[tile // 2, rows, :]
            if tile % 2 == 1:
                value = pltpu.roll(value, LANES // 2, 1)
            for bit in range(5, -1, -1):
                shifted = pltpu.roll(value, 2**bit, 1)
                value = jnp.where((lane & 2 ** (bit + 1)) != 0, shifted, value)
            value = jnp.where((lane & 1) != 0, pltpu.roll(value, 1, 1), value)
            pairs[tile, rows, :] = value
    for x in range(fine.width):
        for no in range(5):
            for tile in range(fine.tiles):
                fine.sent[fine_turn, 1, x + 1, pl.ds(no * fine.tiles + tile, 1), :] = pairs[
                    tile, pl.ds(5 * (x // 2) + no, 1), :
                ]


def kernel(
    sizes,
    coarse_in,
    medium_in,
    fine_in,
    solid_in,
    shear_ref,
    coarse_out,
    medium_out,
    fine_out,
    coarse_own,
    medium_own,
    fine_own,
    solid_own,
    pairs,
    halves,
    *rest,
):
    levels = []
    for t in range(3):
        levels.append(Level(2**t, 2**t, *rest[5 * t : 5 * t + 5]))
    coarse, medium, fine = levels
    own_sem, out_sem = rest[15:17]
    curve_size, level_size = sizes
    me_x, me_y = lax.axis_index("curve"), lax.axis_index("level")
    left, right = lax.rem(me_x + curve_size - 1, curve_size), lax.rem(me_x + 1, curve_size)
    below, above = lax.rem(me_y + level_size - 1, level_size), lax.rem(me_y + 1, level_size)
    around = ((left, right), (below, above), (me_x, me_y))
    at_bottom = me_y == 0
    at_top = me_y == level_size - 1

    def plane_load(x):
        return pltpu.make_async_copy(fine_in.at[:, pl.ds(x, 1)], fine_own.at[:, pl.ds(x, 1)], own_sem.at[x])

    def plane_store(x):
        return pltpu.make_async_copy(fine_own.at[:, pl.ds(x, 1)], fine_out.at[:, pl.ds(x, 1)], out_sem.at[x])

    solid_load = pltpu.make_async_copy(solid_in, solid_own, own_sem.at[4])
    medium_load = pltpu.make_async_copy(medium_in, medium_own, own_sem.at[5])
    coarse_load = pltpu.make_async_copy(coarse_in, coarse_own, own_sem.at[6])
    medium_store = pltpu.make_async_copy(medium_own, medium_out, out_sem.at[4])
    coarse_store = pltpu.make_async_copy(coarse_own, coarse_out, out_sem.at[5])
    solid_load.start()
    for x in range(4):
        plane_load(x).start()
    medium_load.start()
    coarse_load.start()

    barrier = pltpu.get_barrier_semaphore()
    for device in (
        (left, me_y),
        (right, me_y),
        (me_x, below),
        (me_x, above),
        (left, below),
        (left, above),
        (right, below),
        (right, above),
    ):
        pl.semaphore_signal(barrier, inc=1, device_id=device, device_id_type=pl.DeviceIdType.MESH)

    shear = jnp.broadcast_to(shear_ref[...], (ROWS, LANES))
    excess = 1.0 / shear - 0.5
    rates = [1.0 / (2.0**t * excess + 0.5) for t in range(3)]
    everywhere = list(range(1, 19))
    nowhere = []

    def solid_tile(x, tile):
        return solid_own[x, :, tile * LANES : (tile + 1) * LANES] == 1

    def taken(own, x, tile):
        return [own[q, x, :, tile * LANES : (tile + 1) * LANES] for q in range(19)]

    def sweep(level, body):
        def plane(x, carry):
            for tile in range(level.tiles):
                body(x, tile)
            return carry

        if level.width == 1:
            plane(0, 0)
        else:
            lax.fori_loop(0, level.width, plane, 0)

    def put(level, own, turn, blocked, solids):
        def body(x, tile):
            values = level.streamed(turn, x, tile, blocked)
            lanes = slice(tile * LANES, (tile + 1) * LANES)
            for q in range(19):
                value = values[q]
                if solids:
                    value = jnp.where(solid_tile(x, tile), own[q, x, :, lanes], value)
                own[q, x, :, lanes] = value

        return body

    def send(level, turn):
        for copy in level.copies(turn, around):
            copy.start()

    def receive(level, turn):
        for copy in level.copies(turn, around):
            copy.wait_recv()

    def no_wall_above(turn):
        fine.sent[turn, 0] = jnp.full(fine.sent.shape[2:], SOLID, jnp.float32)

    solid_load.wait()

    def first_plane(x, carry):
        plane_load(x).wait()
        for tile in range(fine.tiles):
            fine.keep(0, x, tile, collide(taken(fine_own, x, tile), rates[2], solid_tile(x, tile)))
        return carry

    lax.fori_loop(0, fine.width, first_plane, 0)
    medium_load.wait()
    sweep(medium, lambda x, tile: medium.keep(0, x, tile, collide(taken(medium_own, x, tile), rates[1], None)))
    coarse_load.wait()
    sweep(coarse, lambda x, tile: coarse.keep(0, x, tile, collide(taken(coarse_own, x, tile), rates[0], None)))

    @pl.when(at_top)
    def _():
        no_wall_above(0)
        coalesce(fine, 0, medium, 0, pairs, halves)
        coalesce(medium, 0, coarse, 0, pairs, halves)

    @pl.when(at_bottom)
    def _():
        coarse.sent[0, 1] = jnp.full(coarse.sent.shape[2:], SOLID, jnp.float32)
        explode(medium, 0, fine, 0, pairs, halves)
        explode(coarse, 0, medium, 0, pairs, halves)

    pl.semaphore_wait(barrier, 8)
    send(fine, 0)
    send(medium, 0)
    send(coarse, 0)
    receive(fine, 0)

    def again(turn):
        def body(x, tile):
            values = fine.streamed(turn - 1, x, tile, everywhere)
            fine.keep(turn, x, tile, collide(values, rates[2], solid_tile(x, tile)))

        return body

    sweep(fine, again(1))

    @pl.when(at_top)
    def _():
        no_wall_above(1)

    @pl.when(at_bottom)
    def _():
        fine.sent[1, 1] = fine.sent[0, 1]

    send(fine, 1)
    receive(medium, 0)
    sweep(
        medium,
        lambda x, tile: medium.keep(1, x, tile, collide(medium.streamed(0, x, tile, nowhere), rates[1], None)),
    )
    receive(coarse, 0)
    sweep(coarse, put(coarse, coarse_own, 0, DOWNWARD, False))
    coarse_store.start()

    receive(fine, 1)
    sweep(fine, again(2))

    @pl.when(at_top)
    def _():
        no_wall_above(2)
        coalesce(fine, 2, medium, 1, pairs, halves)

    @pl.when(at_bottom)
    def _():
        explode(medium, 1, fine, 2, pairs, halves)
        medium.sent[1, 1] = medium.sent[0, 1]

    send(fine, 2)
    send(medium, 1)
    receive(fine, 2)

    sweep(fine, again(3))

    @pl.when(at_top)
    def _():
        no_wall_above(3)

    @pl.when(at_bottom)
    def _():
        fine.sent[3, 1] = fine.sent[2, 1]

    send(fine, 3)
    receive(medium, 1)
    sweep(medium, put(medium, medium_own, 1, nowhere, False))
    medium_store.start()
    receive(fine, 3)
    last = put(fine, fine_own, 3, everywhere, True)

    def last_plane(x, carry):
        for tile in range(fine.tiles):
            last(x, tile)
        plane_store(x).start()
        return carry

    lax.fori_loop(0, fine.width, last_plane, 0)
    for level, turns in ((fine, 4), (medium, 2), (coarse, 1)):
        for turn in range(turns):
            for copy in level.copies(turn, around):
                copy.wait_send()
    coarse_store.wait()
    medium_store.wait()
    for x in range(4):
        plane_store(x).wait()


def shards(coarse_pops, medium_pops, fine_pops, solid_cells, shear_rate):
    sizes = (lax.axis_size("curve"), lax.axis_size("level"))
    scratch = [
        pltpu.VMEM(coarse_pops.shape, jnp.float32),
        pltpu.VMEM(medium_pops.shape, jnp.float32),
        pltpu.VMEM(fine_pops.shape, jnp.float32),
        pltpu.VMEM(solid_cells.shape, jnp.int32),
        pltpu.VMEM((4, 16, LANES), jnp.float32),
        pltpu.VMEM((2, 16, LANES), jnp.float32),
    ]
    for t, turns in ((0, 1), (1, 2), (2, 4)):
        width = tiles = 2**t
        lines = (5 * tiles + ROWS - 1) // ROWS * ROWS
        scratch += [
            pltpu.VMEM((turns, 19, width + 2, tiles, ROWS, LANES), jnp.float32),
            pltpu.VMEM((turns, 2, width + 2, lines, LANES), jnp.float32),
            pltpu.VMEM((turns, 2, width + 2, lines, LANES), jnp.float32),
            pltpu.SemaphoreType.DMA((turns, 8)),
            pltpu.SemaphoreType.DMA((turns, 8)),
        ]
    scratch += [pltpu.SemaphoreType.DMA((7,)), pltpu.SemaphoreType.DMA((6,))]
    whole = pl.BlockSpec(memory_space=pl.ANY)
    return pl.pallas_call(
        lambda *refs: kernel(sizes, *refs),
        out_shape=tuple(
            jax.ShapeDtypeStruct(pops.shape, jnp.float32) for pops in (coarse_pops, medium_pops, fine_pops)
        ),
        in_specs=[whole] * 4 + [pl.BlockSpec(memory_space=pltpu.VMEM)],
        out_specs=(whole,) * 3,
        scratch_shapes=scratch,
        compiler_params=pltpu.CompilerParams(
            collective_id=0, has_side_effects=True, vmem_limit_bytes=48 * 1024 * 1024
        ),
    )(coarse_pops, medium_pops, fine_pops, solid_cells, shear_rate)


def solution(mesh):
    lattice = P(None, "curve", "level", None)
    return jax.shard_map(
        shards,
        mesh=mesh,
        in_specs=(lattice, lattice, lattice, P("curve", "level", None), P("curve", "level")),
        out_specs=(lattice, lattice, lattice),
        check_vma=False,
    )
```

profile of v0, /device:TPU:1, one launch (start us, length us, event | category | flops | bytes accessed | tf_op | source)
XLA Modules:
  0.0 55.0 jit_solution(16488656268331002459)
XLA Ops:
  1.3 0.0 copy-start
  1.3 1.3 %copy-done = f32[19,4,8,512]{3,2,1,0:T(8,128)S(1)} copy-done((f32[19,4,8,512]{3,2,1,0:T(8,128)S(1)}, f32[19,4,8,512]{3,2,1,0:T(8,128)}, u32[]{:S(2)}) %copy-start) | copy-done | bytes 1245208
  2.6 0.0 copy-start.1
  2.6 1.0 %copy-done.1 = f32[19,2,8,256]{3,2,1,0:T(8,128)S(1)} copy-done((f32[19,2,8,256]{3,2,1,0:T(8,128)S(1)}, f32[19,2,8,256]{3,2,1,0:T(8,128)}, u32[]{:S(2)}) %copy-start.1) | copy-done | bytes 311320
  3.5 0.0 copy-start.2
  3.5 0.9 %copy-done.2 = f32[19,1,8,128]{3,2,1,0:T(8,128)S(1)} copy-done((f32[19,1,8,128]{3,2,1,0:T(8,128)S(1)}, f32[19,1,8,128]{3,2,1,0:T(8,128)}, u32[]{:S(2)}) %copy-start.2) | copy-done | bytes 77848
  4.4 0.0 copy-start.3
  4.4 0.8 %copy-done.3 = s32[4,8,512]{2,1,0:T(8,128)S(1)} copy-done((s32[4,8,512]{2,1,0:T(8,128)S(1)}, s32[4,8,512]{2,1,0:T(8,128)}, u32[]{:S(2)}) %copy-start.3) | copy-done | bytes 65560
  5.3 47.4 %shard_map.76 = (f32[19,1,8,128]{3,2,1,0:T(8,128)S(1)}, f32[19,2,8,256]{3,2,1,0:T(8,128)S(1)}, f32[19,4,8,512]{3,2,1,0:T(8,128)S(1)}) custom-call(f32[19,1,8,128]{3,2,1,0:T(8,128)S(1)} %copy-done.2, f32[19,2,8,256]{3,2,1,0:T(8,128)S(1)} %copy-done.1, f32[19,4,8,512]{3,2,1,0:T(8,128)S(1)} %copy-done, s32[4,8,512]{2,1,0:T(8,128)S(1)} %copy-done.3, ...), custom_call_target="tpu_custom_call" | custom-call | tf_op jit(solution)/shard_map/pallas_call | solution.py:497
  52.6 0.6 %copy.12 = f32[19,1,8,128]{3,2,1,0:T(8,128)} copy(f32[19,1,8,128]{3,2,1,0:T(8,128)S(1)} %get-tuple-element.6) | data formatting | bytes 155648
  53.3 0.7 %copy.13 = f32[19,2,8,256]{3,2,1,0:T(8,128)} copy(f32[19,2,8,256]{3,2,1,0:T(8,128)S(1)} %get-tuple-element.7) | data formatting | bytes 622592
  54.0 1.0 %copy.14 = f32[19,4,8,512]{3,2,1,0:T(8,128)} copy(f32[19,4,8,512]{3,2,1,0:T(8,128)S(1)} %get-tuple-element.8) | data formatting | bytes 2490368
Async XLA Ops:
  1.3 1.3 %copy-start = (f32[19,4,8,512]{3,2,1,0:T(8,128)S(1)}, f32[19,4,8,512]{3,2,1,0:T(8,128)}, u32[]{:S(2)}) copy-start(f32[19,4,8,512]{3,2,1,0:T(8,128)} %refs_2_.1) | copy-start | bytes 3735556
  2.6 1.0 %copy-start.1 = (f32[19,2,8,256]{3,2,1,0:T(8,128)S(1)}, f32[19,2,8,256]{3,2,1,0:T(8,128)}, u32[]{:S(2)}) copy-start(f32[19,2,8,256]{3,2,1,0:T(8,128)} %refs_1_.1) | copy-start | bytes 933892
  3.5 0.9 %copy-start.2 = (f32[19,1,8,128]{3,2,1,0:T(8,128)S(1)}, f32[19,1,8,128]{3,2,1,0:T(8,128)}, u32[]{:S(2)}) copy-start(f32[19,1,8,128]{3,2,1,0:T(8,128)} %refs_0_.1) | copy-start | bytes 233476
  4.4 0.8 %copy-start.3 = (s32[4,8,512]{2,1,0:T(8,128)S(1)}, s32[4,8,512]{2,1,0:T(8,128)}, u32[]{:S(2)}) copy-start(s32[4,8,512]{2,1,0:T(8,128)} %refs_3_.1) | copy-start | bytes 196612
where the time goes:
time: 55.7 us; the launch traced here: 55 us
  Pallas kernels  47.4 us (85%)
  local copies, waits for them, and re-layouts  6.37 us (11%)
  between operations  1.3 us (2%)
    pallas_call x1, Pallas kernels, shards(): pl.pallas_call(lambda *refs: kernel(sizes, *refs), out_shape=tuple((jax.S...  47.4 us
    unnamed x11, local copies, waits for them, and re-layouts  6.37 us

commit v1 on v0

--- a/solution.py
+++ b/solution.py
@@ -34,6 +34,9 @@
 DOWNWARD = [9, 4, 8, 16, 18]
 ROWS = 8
 LANES = 128
+SUBSTEPS = 4
+EVERY = tuple(range(1, 19))
+CORNERS_FIRST = (4, 5, 6, 7, 0, 1, 2, 3)
 SOLID = float("nan")
 
 
@@ -129,7 +132,7 @@
         (left, right), (below, above), (me_x, me_y) = around
 
         def copy(no, source, target, device):
-            return pltpu.make_async_remote_copy(
+            return lambda: pltpu.make_async_remote_copy(
                 src_ref=source,
                 dst_ref=target,
                 send_sem=self.send_sem.at[turn, no],
@@ -194,6 +197,10 @@
                 value = jnp.where(value != value, relaxed[turn, PLACE[OPPOSITE[q]], x + 1, tile], value)
             values.append(value)
         return values
+
+
+def solid_tile(solid, x, tile):
+    return solid[x, :, tile * LANES : (tile + 1) * LANES] == 1
 
 
 def coalesce(fine, fine_turn, coarse, coarse_turn, pairs, halves):
@@ -228,7 +235,7 @@
                 ]
 
 
-def explode(coarse, coarse_turn, fine, fine_turn, pairs, halves):
+def explode(coarse, coarse_turn, target, fine, pairs, halves):
     lane = lax.broadcasted_iota(jnp.int32, (ROWS, LANES), 1)
     for x in range(coarse.width):
         for no, q in enumerate(DOWNWARD):
@@ -250,7 +257,7 @@
     for x in range(fine.width):
         for no in range(5):
             for tile in range(fine.tiles):
-                fine.sent[fine_turn, 1, x + 1, pl.ds(no * fine.tiles + tile, 1), :] = pairs[
+                target[x + 1, pl.ds(no * fine.tiles + tile, 1), :] = pairs[
                     tile, pl.ds(5 * (x // 2) + no, 1), :
                 ]
 
@@ -262,22 +269,21 @@
     fine_in,
     solid_in,
     shear_ref,
-    coarse_out,
-    medium_out,
-    fine_out,
     coarse_own,
     medium_own,
     fine_own,
     solid_own,
+    fine_relaxed,
+    fine_came,
     pairs,
     halves,
+    exploded,
+    own_sem,
     *rest,
 ):
-    levels = []
-    for t in range(3):
-        levels.append(Level(2**t, 2**t, *rest[5 * t : 5 * t + 5]))
-    coarse, medium, fine = levels
-    own_sem, out_sem = rest[15:17]
+    coarse = Level(1, 1, *rest[:5])
+    medium = Level(2, 2, *rest[5:10])
+    fine = Level(4, 4, fine_relaxed, rest[10], fine_came, *rest[11:])
     curve_size, level_size = sizes
     me_x, me_y = lax.axis_index("curve"), lax.axis_index("level")
     left, right = lax.rem(me_x + curve_size - 1, curve_size), lax.rem(me_x + 1, curve_size)
@@ -289,18 +295,15 @@
     def plane_load(x):
         return pltpu.make_async_copy(fine_in.at[:, pl.ds(x, 1)], fine_own.at[:, pl.ds(x, 1)], own_sem.at[x])
 
-    def plane_store(x):
-        return pltpu.make_async_copy(fine_own.at[:, pl.ds(x, 1)], fine_out.at[:, pl.ds(x, 1)], out_sem.at[x])
-
     solid_load = pltpu.make_async_copy(solid_in, solid_own, own_sem.at[4])
     medium_load = pltpu.make_async_copy(medium_in, medium_own, own_sem.at[5])
     coarse_load = pltpu.make_async_copy(coarse_in, coarse_own, own_sem.at[6])
-    medium_store = pltpu.make_async_copy(medium_own, medium_out, out_sem.at[4])
-    coarse_store = pltpu.make_async_copy(coarse_own, coarse_out, out_sem.at[5])
+    medium_load.start()
+    for x in (0, 3):
+        plane_load(x).start()
     solid_load.start()
-    for x in range(4):
+    for x in (1, 2):
         plane_load(x).start()
-    medium_load.start()
     coarse_load.start()
 
     barrier = pltpu.get_barrier_semaphore()
@@ -319,11 +322,6 @@
     shear = jnp.broadcast_to(shear_ref[...], (ROWS, LANES))
     excess = 1.0 / shear - 0.5
     rates = [1.0 / (2.0**t * excess + 0.5) for t in range(3)]
-    everywhere = list(range(1, 19))
-    nowhere = []
-
-    def solid_tile(x, tile):
-        return solid_own[x, :, tile * LANES : (tile + 1) * LANES] == 1
 
     def taken(own, x, tile):
         return [own[q, x, :, tile * LANES : (tile + 1) * LANES] for q in range(19)]
@@ -339,173 +337,198 @@
         else:
             lax.fori_loop(0, level.width, plane, 0)
 
-    def put(level, own, turn, blocked, solids):
+    def put(level, own, turn, blocked):
         def body(x, tile):
             values = level.streamed(turn, x, tile, blocked)
-            lanes = slice(tile * LANES, (tile + 1) * LANES)
             for q in range(19):
-                value = values[q]
-                if solids:
-                    value = jnp.where(solid_tile(x, tile), own[q, x, :, lanes], value)
-                own[q, x, :, lanes] = value
+                own[q, x, :, tile * LANES : (tile + 1) * LANES] = values[q]
 
         return body
 
-    def send(level, turn):
-        for copy in level.copies(turn, around):
-            copy.start()
+    def send(level, turn, which):
+        copies = level.copies(turn, around)
+        for no in which:
+            copies[no]().start()
 
     def receive(level, turn):
         for copy in level.copies(turn, around):
-            copy.wait_recv()
-
-    def no_wall_above(turn):
-        fine.sent[turn, 0] = jnp.full(fine.sent.shape[2:], SOLID, jnp.float32)
+            copy().wait_recv()
+
+    def sent_off(level, turn):
+        for copy in level.copies(turn, around):
+            copy().wait_send()
+
+    def wall_above(turn, x):
+        fine.sent[turn, 0, x + 1] = jnp.full(fine.sent.shape[3:], SOLID, jnp.float32)
+
+    def edges(turn, x):
+        @pl.when(at_top)
+        def _():
+            wall_above(turn, x)
+
+        @pl.when(at_bottom)
+        def _():
+            fine.sent[turn, 1, x + 1] = exploded[x + 1]
+
+    def fine_pass(turn, relax):
+        def plane(step, carry):
+            x = jnp.where(step < 2, 3 * step, step - 1)
+            relax(x)
+            edges(turn, x)
+
+            @pl.when(step == 1)
+            def _():
+                send(fine, turn, (4, 5, 6, 7, 0, 1))
+
+            return carry
+
+        lax.fori_loop(0, fine.width, plane, 0)
+        send(fine, turn, (2, 3))
+
+    medium_load.wait()
+    sweep(medium, lambda x, tile: medium.keep(0, x, tile, collide(taken(medium_own, x, tile), rates[1], None)))
+
+    @pl.when(at_bottom)
+    def _():
+        explode(medium, 0, exploded, fine, pairs, halves)
 
     solid_load.wait()
-
-    def first_plane(x, carry):
+    pl.semaphore_wait(barrier, 8)
+
+    def first(x):
         plane_load(x).wait()
         for tile in range(fine.tiles):
-            fine.keep(0, x, tile, collide(taken(fine_own, x, tile), rates[2], solid_tile(x, tile)))
-        return carry
-
-    lax.fori_loop(0, fine.width, first_plane, 0)
-    medium_load.wait()
-    sweep(medium, lambda x, tile: medium.keep(0, x, tile, collide(taken(medium_own, x, tile), rates[1], None)))
+            fine.keep(0, x, tile, collide(taken(fine_own, x, tile), rates[2], solid_tile(solid_own, x, tile)))
+
+    fine_pass(0, first)
     coarse_load.wait()
     sweep(coarse, lambda x, tile: coarse.keep(0, x, tile, collide(taken(coarse_own, x, tile), rates[0], None)))
 
     @pl.when(at_top)
     def _():
-        no_wall_above(0)
         coalesce(fine, 0, medium, 0, pairs, halves)
         coalesce(medium, 0, coarse, 0, pairs, halves)
 
     @pl.when(at_bottom)
     def _():
         coarse.sent[0, 1] = jnp.full(coarse.sent.shape[2:], SOLID, jnp.float32)
-        explode(medium, 0, fine, 0, pairs, halves)
-        explode(coarse, 0, medium, 0, pairs, halves)
-
-    pl.semaphore_wait(barrier, 8)
-    send(fine, 0)
-    send(medium, 0)
-    send(coarse, 0)
-    receive(fine, 0)
-
-    def again(turn):
-        def body(x, tile):
-            values = fine.streamed(turn - 1, x, tile, everywhere)
-            fine.keep(turn, x, tile, collide(values, rates[2], solid_tile(x, tile)))
-
-        return body
-
-    sweep(fine, again(1))
-
-    @pl.when(at_top)
-    def _():
-        no_wall_above(1)
-
-    @pl.when(at_bottom)
-    def _():
-        fine.sent[1, 1] = fine.sent[0, 1]
-
-    send(fine, 1)
-    receive(medium, 0)
-    sweep(
-        medium,
-        lambda x, tile: medium.keep(1, x, tile, collide(medium.streamed(0, x, tile, nowhere), rates[1], None)),
-    )
-    receive(coarse, 0)
-    sweep(coarse, put(coarse, coarse_own, 0, DOWNWARD, False))
-    coarse_store.start()
-
-    receive(fine, 1)
-    sweep(fine, again(2))
-
-    @pl.when(at_top)
-    def _():
-        no_wall_above(2)
-        coalesce(fine, 2, medium, 1, pairs, halves)
-
-    @pl.when(at_bottom)
-    def _():
-        explode(medium, 1, fine, 2, pairs, halves)
-        medium.sent[1, 1] = medium.sent[0, 1]
-
-    send(fine, 2)
-    send(medium, 1)
-    receive(fine, 2)
-
-    sweep(fine, again(3))
-
-    @pl.when(at_top)
-    def _():
-        no_wall_above(3)
-
-    @pl.when(at_bottom)
-    def _():
-        fine.sent[3, 1] = fine.sent[2, 1]
-
-    send(fine, 3)
+        explode(coarse, 0, medium.sent.at[0, 1], medium, pairs, halves)
+
+    send(medium, 0, CORNERS_FIRST)
+    send(coarse, 0, CORNERS_FIRST)
+
+    def substep(turn, carry):
+        receive(fine, turn - 1)
+
+        def again(x):
+            for tile in range(fine.tiles):
+                values = fine.streamed(turn - 1, x, tile, EVERY)
+                fine.keep(turn, x, tile, collide(values, rates[2], solid_tile(solid_own, x, tile)))
+
+        fine_pass(turn, again)
+
+        @pl.when(turn == 1)
+        def _():
+            receive(medium, 0)
+            sweep(
+                medium,
+                lambda x, tile: medium.keep(1, x, tile, collide(medium.streamed(0, x, tile, ()), rates[1], None)),
+            )
+
+            @pl.when(at_bottom)
+            def _():
+                explode(medium, 1, exploded, fine, pairs, halves)
+                medium.sent[1, 1] = medium.sent[0, 1]
+
+            receive(coarse, 0)
+            sweep(coarse, put(coarse, coarse_own, 0, DOWNWARD))
+
+        @pl.when(turn == 2)
+        def _():
+            @pl.when(at_top)
+            def _():
+                coalesce(fine, 2, medium, 1, pairs, halves)
+
+            send(medium, 1, CORNERS_FIRST)
+
+        return carry
+
+    lax.fori_loop(1, SUBSTEPS, substep, 0)
     receive(medium, 1)
-    sweep(medium, put(medium, medium_own, 1, nowhere, False))
-    medium_store.start()
-    receive(fine, 3)
-    last = put(fine, fine_own, 3, everywhere, True)
-
-    def last_plane(x, carry):
+    sweep(medium, put(medium, medium_own, 1, ()))
+    sent_off(coarse, 0)
+    sent_off(medium, 0)
+    sent_off(medium, 1)
+    for turn in range(SUBSTEPS - 1):
+        sent_off(fine, turn)
+    receive(fine, SUBSTEPS - 1)
+    sent_off(fine, SUBSTEPS - 1)
+
+
+def finish(coarse, medium, fine_pops, solid, fine_relaxed, fine_came, coarse_out, medium_out, fine_out, own, sem):
+    others = [
+        pltpu.make_async_copy(source, target, sem.at[no])
+        for no, (source, target) in enumerate(((medium, medium_out), (coarse, coarse_out)))
+    ]
+    for copy in others:
+        copy.start()
+
+    def plane_store(x):
+        return pltpu.make_async_copy(own.at[:, pl.ds(x, 1)], fine_out.at[:, pl.ds(x, 1)], sem.at[2 + x])
+
+    fine = Level(4, 4, fine_relaxed, None, fine_came, None, None)
+
+    def plane(x, carry):
         for tile in range(fine.tiles):
-            last(x, tile)
+            values = fine.streamed(SUBSTEPS - 1, x, tile, EVERY)
+            lanes = slice(tile * LANES, (tile + 1) * LANES)
+            for q in range(19):
+                own[q, x, :, lanes] = jnp.where(solid_tile(solid, x, tile), fine_pops[q, x, :, lanes], values[q])
         plane_store(x).start()
         return carry
 
-    lax.fori_loop(0, fine.width, last_plane, 0)
-    for level, turns in ((fine, 4), (medium, 2), (coarse, 1)):
-        for turn in range(turns):
-            for copy in level.copies(turn, around):
-                copy.wait_send()
-    coarse_store.wait()
-    medium_store.wait()
-    for x in range(4):
+    lax.fori_loop(0, fine.width, plane, 0)
+    for copy in others:
+        copy.wait()
+    for x in range(fine.width):
         plane_store(x).wait()
 
 
 def shards(coarse_pops, medium_pops, fine_pops, solid_cells, shear_rate):
     sizes = (lax.axis_size("curve"), lax.axis_size("level"))
     scratch = [
-        pltpu.VMEM(coarse_pops.shape, jnp.float32),
-        pltpu.VMEM(medium_pops.shape, jnp.float32),
-        pltpu.VMEM(fine_pops.shape, jnp.float32),
-        pltpu.VMEM(solid_cells.shape, jnp.int32),
         pltpu.VMEM((4, 16, LANES), jnp.float32),
         pltpu.VMEM((2, 16, LANES), jnp.float32),
+        pltpu.VMEM((6, 24, LANES), jnp.float32),
+        pltpu.SemaphoreType.DMA((7,)),
     ]
-    for t, turns in ((0, 1), (1, 2), (2, 4)):
+    for t, turns in ((0, 1), (1, 2), (2, SUBSTEPS)):
         width = tiles = 2**t
         lines = (5 * tiles + ROWS - 1) // ROWS * ROWS
-        scratch += [
-            pltpu.VMEM((turns, 19, width + 2, tiles, ROWS, LANES), jnp.float32),
-            pltpu.VMEM((turns, 2, width + 2, lines, LANES), jnp.float32),
-            pltpu.VMEM((turns, 2, width + 2, lines, LANES), jnp.float32),
-            pltpu.SemaphoreType.DMA((turns, 8)),
-            pltpu.SemaphoreType.DMA((turns, 8)),
-        ]
-    scratch += [pltpu.SemaphoreType.DMA((7,)), pltpu.SemaphoreType.DMA((6,))]
-    whole = pl.BlockSpec(memory_space=pl.ANY)
-    return pl.pallas_call(
+        relaxed = pltpu.VMEM((turns, 19, width + 2, tiles, ROWS, LANES), jnp.float32)
+        edge_rows = pltpu.VMEM((turns, 2, width + 2, lines, LANES), jnp.float32)
+        scratch += [edge_rows] if t == 2 else [relaxed, edge_rows, edge_rows]
+        scratch += [pltpu.SemaphoreType.DMA((turns, 8))] * 2
+    given = (coarse_pops, medium_pops, fine_pops, solid_cells)
+    in_vmem = pl.BlockSpec(memory_space=pltpu.VMEM)
+    held = pl.pallas_call(
         lambda *refs: kernel(sizes, *refs),
-        out_shape=tuple(
-            jax.ShapeDtypeStruct(pops.shape, jnp.float32) for pops in (coarse_pops, medium_pops, fine_pops)
-        ),
-        in_specs=[whole] * 4 + [pl.BlockSpec(memory_space=pltpu.VMEM)],
-        out_specs=(whole,) * 3,
+        out_shape=tuple(pltpu.VMEM(array.shape, array.dtype) for array in given) + (relaxed, edge_rows),
+        in_specs=[pl.BlockSpec(memory_space=pltpu.HBM)] * 4 + [in_vmem],
+        out_specs=(in_vmem,) * 6,
         scratch_shapes=scratch,
         compiler_params=pltpu.CompilerParams(
-            collective_id=0, has_side_effects=True, vmem_limit_bytes=48 * 1024 * 1024
+            collective_id=0, has_side_effects=True, vmem_limit_bytes=24 * 1024 * 1024
         ),
-    )(coarse_pops, medium_pops, fine_pops, solid_cells, shear_rate)
+    )(*[pltpu.with_memory_space_constraint(array, pltpu.HBM) for array in given], shear_rate)
+    return pl.pallas_call(
+        finish,
+        out_shape=tuple(jax.ShapeDtypeStruct(pops.shape, jnp.float32) for pops in given[:3]),
+        in_specs=[in_vmem] * 6,
+        out_specs=(pl.BlockSpec(memory_space=pl.ANY),) * 3,
+        scratch_shapes=[pltpu.VMEM(fine_pops.shape, jnp.float32), pltpu.SemaphoreType.DMA((6,))],
+        compiler_params=pltpu.CompilerParams(vmem_limit_bytes=24 * 1024 * 1024),
+    )(*held)
 
 
 def solution(mesh):

time: 55.7 us -> 47.5 us (0.85)
  local copies, waits for them, and re-layouts: 6.37 us -> 0 us
  Pallas kernels: 47.4 us -> 46.1 us
    unnamed x11 -> x0, local copies, waits for them, and re-layouts: 6.37 us -> none
    pallas_call x1 -> x2, Pallas kernels: 47.4 us -> 46.1 us  [the longest x1 44.7 us: shards(): pl.pallas_call(lambda *refs: kernel(sizes, *refs), out_shape=tuple((pltpu...]
where the time goes in v1:
time: 47.5 us; the launch traced here: 47.3 us
  Pallas kernels  46.1 us (97%)
  between operations  1.29 us (3%)
    pallas_call x1, Pallas kernels, shards(): pl.pallas_call(lambda *refs: kernel(sizes, *refs), out_shape=tuple((pltpu...  44.7 us
    pallas_call x1, Pallas kernels, shards(): pl.pallas_call(finish, out_shape=tuple((jax.ShapeDtypeStruct(pops.shape,...  1.32 us

profile of v1, /device:TPU:1, one launch (start us, length us, event | category | flops | bytes accessed | tf_op | source)
XLA Modules:
  0.0 47.3 jit_solution(5108532025073547641)
XLA Ops:
  1.3 44.7 %shard_map.76 = (f32[19,1,8,128]{3,2,1,0:T(8,128)S(1)}, f32[19,2,8,256]{3,2,1,0:T(8,128)S(1)}, f32[19,4,8,512]{3,2,1,0:T(8,128)S(1)}, s32[4,8,512]{2,1,0:T(8,128...) custom-call(f32[19,1,8,128]{3,2,1,0:T(8,128)} %refs_0_.1, f32[19,2,8,256]{3,2,1,0:T(8,128)} %refs_1_.1, ...), custom_call_target="tpu_custom_call" | custom-call | tf_op jit(solution)/shard_map/pallas_call | solution.py:514
  46.0 1.3 %shard_map.77 = (f32[19,1,8,128]{3,2,1,0:T(8,128)}, f32[19,2,8,256]{3,2,1,0:T(8,128)}, f32[19,4,8,512]{3,2,1,0:T(8,128)}) custom-call(f32[19,1,8,128]{3,2,1,0:T(8,128)S(1)} %get-tuple-element.9.coarse, f32[19,2,8,256]{3,2,1,0:T(8,128)S(1)} %get-tuple-element.10.medium, f32[19,4,8,512]{3,2,1,0:T(8,128)S(1)} %get-tuple-element.11.fine_pops, ...), custom_call_target="tpu_custom_call" | custom-call | tf_op jit(solution)/shard_map/pallas_call | solution.py:524

commit v2 on v1

--- a/solution.py
+++ b/solution.py
@@ -36,6 +36,9 @@
 LANES = 128
 SUBSTEPS = 4
 EVERY = tuple(range(1, 19))
+FROM_LEFT = (4, 5, 0)
+FROM_RIGHT = (6, 7, 1)
+ROWS_ONLY = (2, 3)
 CORNERS_FIRST = (4, 5, 6, 7, 0, 1, 2, 3)
 SOLID = float("nan")
 
@@ -153,6 +156,7 @@
             result.append(
                 copy(4 + way, sent.at[turn, way, width, first], came.at[turn, way, 0, first], (right, beyond))
             )
+        for way, beyond in ((0, above), (1, below)):
             result.append(
                 copy(6 + way, sent.at[turn, way, 1, last], came.at[turn, way, width + 1, last], (left, beyond))
             )
@@ -350,9 +354,10 @@
         for no in which:
             copies[no]().start()
 
-    def receive(level, turn):
-        for copy in level.copies(turn, around):
-            copy().wait_recv()
+    def receive(level, turn, which=CORNERS_FIRST):
+        copies = level.copies(turn, around)
+        for no in which:
+            copies[no]().wait_recv()
 
     def sent_off(level, turn):
         for copy in level.copies(turn, around):
@@ -371,19 +376,27 @@
             fine.sent[turn, 1, x + 1] = exploded[x + 1]
 
     def fine_pass(turn, relax):
-        def plane(step, carry):
-            x = jnp.where(step < 2, 3 * step, step - 1)
+        def plane(x):
             relax(x)
             edges(turn, x)
 
-            @pl.when(step == 1)
-            def _():
-                send(fine, turn, (4, 5, 6, 7, 0, 1))
-
+        if turn > 0:
+            receive(fine, turn - 1, ROWS_ONLY + FROM_LEFT)
+        plane(0)
+        if turn == 0:
+            pl.semaphore_wait(barrier, 8)
+        send(fine, turn, FROM_RIGHT)
+        if turn > 0:
+            receive(fine, turn - 1, FROM_RIGHT)
+        plane(3)
+        send(fine, turn, FROM_LEFT)
+
+        def inner(x, carry):
+            plane(x)
             return carry
 
-        lax.fori_loop(0, fine.width, plane, 0)
-        send(fine, turn, (2, 3))
+        lax.fori_loop(1, 3, inner, 0)
+        send(fine, turn, ROWS_ONLY)
 
     medium_load.wait()
     sweep(medium, lambda x, tile: medium.keep(0, x, tile, collide(taken(medium_own, x, tile), rates[1], None)))
@@ -393,7 +406,6 @@
         explode(medium, 0, exploded, fine, pairs, halves)
 
     solid_load.wait()
-    pl.semaphore_wait(barrier, 8)
 
     def first(x):
         plane_load(x).wait()
@@ -417,43 +429,38 @@
     send(medium, 0, CORNERS_FIRST)
     send(coarse, 0, CORNERS_FIRST)
 
-    def substep(turn, carry):
-        receive(fine, turn - 1)
-
-        def again(x):
+    def again(turn):
+        def relax(x):
             for tile in range(fine.tiles):
                 values = fine.streamed(turn - 1, x, tile, EVERY)
                 fine.keep(turn, x, tile, collide(values, rates[2], solid_tile(solid_own, x, tile)))
 
-        fine_pass(turn, again)
-
-        @pl.when(turn == 1)
-        def _():
-            receive(medium, 0)
-            sweep(
-                medium,
-                lambda x, tile: medium.keep(1, x, tile, collide(medium.streamed(0, x, tile, ()), rates[1], None)),
-            )
-
-            @pl.when(at_bottom)
-            def _():
-                explode(medium, 1, exploded, fine, pairs, halves)
-                medium.sent[1, 1] = medium.sent[0, 1]
-
-            receive(coarse, 0)
-            sweep(coarse, put(coarse, coarse_own, 0, DOWNWARD))
-
-        @pl.when(turn == 2)
-        def _():
-            @pl.when(at_top)
-            def _():
-                coalesce(fine, 2, medium, 1, pairs, halves)
-
-            send(medium, 1, CORNERS_FIRST)
-
-        return carry
-
-    lax.fori_loop(1, SUBSTEPS, substep, 0)
+        fine_pass(turn, relax)
+
+    again(1)
+    receive(medium, 0)
+    sweep(
+        medium,
+        lambda x, tile: medium.keep(1, x, tile, collide(medium.streamed(0, x, tile, ()), rates[1], None)),
+    )
+
+    @pl.when(at_bottom)
+    def _():
+        explode(medium, 1, exploded, fine, pairs, halves)
+        medium.sent[1, 1] = medium.sent[0, 1]
+
+    receive(coarse, 0)
+    sweep(coarse, put(coarse, coarse_own, 0, DOWNWARD))
+
+    again(2)
+
+    @pl.when(at_top)
+    def _():
+        coalesce(fine, 2, medium, 1, pairs, halves)
+
+    send(medium, 1, CORNERS_FIRST)
+
+    again(3)
     receive(medium, 1)
     sweep(medium, put(medium, medium_own, 1, ()))
     sent_off(coarse, 0)
@@ -461,37 +468,44 @@
     sent_off(medium, 1)
     for turn in range(SUBSTEPS - 1):
         sent_off(fine, turn)
-    receive(fine, SUBSTEPS - 1)
-    sent_off(fine, SUBSTEPS - 1)
-
-
-def finish(coarse, medium, fine_pops, solid, fine_relaxed, fine_came, coarse_out, medium_out, fine_out, own, sem):
-    others = [
-        pltpu.make_async_copy(source, target, sem.at[no])
-        for no, (source, target) in enumerate(((medium, medium_out), (coarse, coarse_out)))
-    ]
-    for copy in others:
-        copy.start()
-
-    def plane_store(x):
-        return pltpu.make_async_copy(own.at[:, pl.ds(x, 1)], fine_out.at[:, pl.ds(x, 1)], sem.at[2 + x])
-
-    fine = Level(4, 4, fine_relaxed, None, fine_came, None, None)
-
-    def plane(x, carry):
+
+    receive(fine, SUBSTEPS - 1, ROWS_ONLY)
+
+    def inner(x, carry):
         for tile in range(fine.tiles):
             values = fine.streamed(SUBSTEPS - 1, x, tile, EVERY)
             lanes = slice(tile * LANES, (tile + 1) * LANES)
+            solid = solid_tile(solid_own, x, tile)
             for q in range(19):
-                own[q, x, :, lanes] = jnp.where(solid_tile(solid, x, tile), fine_pops[q, x, :, lanes], values[q])
-        plane_store(x).start()
+                fine_own[q, x, :, lanes] = jnp.where(solid, fine_own[q, x, :, lanes], values[q])
         return carry
 
-    lax.fori_loop(0, fine.width, plane, 0)
-    for copy in others:
+    lax.fori_loop(1, 3, inner, 0)
+    receive(fine, SUBSTEPS - 1, FROM_LEFT + FROM_RIGHT)
+    sent_off(fine, SUBSTEPS - 1)
+
+
+def finish(coarse, medium, inner, fine_relaxed, fine_came, coarse_out, medium_out, fine_out, outer, sem):
+    planes = pl.ds(1, 2)
+    done = [
+        pltpu.make_async_copy(source, target, sem.at[no])
+        for no, (source, target) in enumerate(
+            ((inner.at[:, planes], fine_out.at[:, planes]), (medium, medium_out), (coarse, coarse_out))
+        )
+    ]
+    for copy in done:
+        copy.start()
+    fine = Level(4, 4, fine_relaxed, None, fine_came, None, None)
+    for no, x in enumerate((0, 3)):
+        for tile in range(fine.tiles):
+            values = fine.streamed(SUBSTEPS - 1, x, tile, EVERY)
+            for q in range(19):
+                outer[q, no, :, tile * LANES : (tile + 1) * LANES] = values[q]
+        store = pltpu.make_async_copy(outer.at[:, pl.ds(no, 1)], fine_out.at[:, pl.ds(x, 1)], sem.at[3 + no])
+        store.start()
+        done.append(store)
+    for copy in done:
         copy.wait()
-    for x in range(fine.width):
-        plane_store(x).wait()
 
 
 def shards(coarse_pops, medium_pops, fine_pops, solid_cells, shear_rate):
@@ -524,11 +538,11 @@
     return pl.pallas_call(
         finish,
         out_shape=tuple(jax.ShapeDtypeStruct(pops.shape, jnp.float32) for pops in given[:3]),
-        in_specs=[in_vmem] * 6,
+        in_specs=[in_vmem] * 5,
         out_specs=(pl.BlockSpec(memory_space=pl.ANY),) * 3,
-        scratch_shapes=[pltpu.VMEM(fine_pops.shape, jnp.float32), pltpu.SemaphoreType.DMA((6,))],
+        scratch_shapes=[pltpu.VMEM((19, 2, ROWS, 4 * LANES), jnp.float32), pltpu.SemaphoreType.DMA((5,))],
         compiler_params=pltpu.CompilerParams(vmem_limit_bytes=24 * 1024 * 1024),
-    )(*held)
+    )(*held[:3], *held[4:])
 
 
 def solution(mesh):

time: 47.5 us -> 45.4 us (0.956)
  Pallas kernels: 46.1 us -> 44 us
    pallas_call x1, Pallas kernels: 44.7 us -> 42.7 us  [shards(): pl.pallas_call(lambda *refs: kernel(sizes, *refs), out_shape=tuple((pltpu...]
where the time goes in v2:
time: 45.4 us; the launch traced here: 45.2 us
  Pallas kernels  44 us (97%)
  between operations  1.29 us (3%)
    pallas_call x1, Pallas kernels, shards(): pl.pallas_call(lambda *refs: kernel(sizes, *refs), out_shape=tuple((pltpu...  42.7 us
    pallas_call x1, Pallas kernels, shards(): pl.pallas_call(finish, out_shape=tuple((jax.ShapeDtypeStruct(pops.shape,...  1.21 us

profile of v2, /device:TPU:1, one launch (start us, length us, event | category | flops | bytes accessed | tf_op | source)
XLA Modules:
  0.0 45.2 jit_solution(14291096387899681433)
XLA Ops:
  1.3 42.7 %shard_map.76 = (f32[19,1,8,128]{3,2,1,0:T(8,128)S(1)}, f32[19,2,8,256]{3,2,1,0:T(8,128)S(1)}, f32[19,4,8,512]{3,2,1,0:T(8,128)S(1)}, s32[4,8,512]{2,1,0:T(8,128...) custom-call(f32[19,1,8,128]{3,2,1,0:T(8,128)} %refs_0_.1, f32[19,2,8,256]{3,2,1,0:T(8,128)} %refs_1_.1, ...), custom_call_target="tpu_custom_call" | custom-call | tf_op jit(solution)/shard_map/pallas_call | solution.py:528
  44.0 1.2 %shard_map.77 = (f32[19,1,8,128]{3,2,1,0:T(8,128)}, f32[19,2,8,256]{3,2,1,0:T(8,128)}, f32[19,4,8,512]{3,2,1,0:T(8,128)}) custom-call(f32[19,1,8,128]{3,2,1,0:T(8,128)S(1)} %get-tuple-element.8.coarse, f32[19,2,8,256]{3,2,1,0:T(8,128)S(1)} %get-tuple-element.9.medium, f32[19,4,8,512]{3,2,1,0:T(8,128)S(1)} %get-tuple-element.10.inner, ...), custom_call_target="tpu_custom_call" | custom-call | tf_op jit(solution)/shard_map/pallas_call | solution.py:538

commit v3 on v2

--- a/solution.py
+++ b/solution.py
@@ -39,6 +39,8 @@
 FROM_LEFT = (4, 5, 0)
 FROM_RIGHT = (6, 7, 1)
 ROWS_ONLY = (2, 3)
+ROWS_0 = (8, 9)
+ROWS_3 = (10, 11)
 CORNERS_FIRST = (4, 5, 6, 7, 0, 1, 2, 3)
 SOLID = float("nan")
 
@@ -144,7 +146,8 @@
                 device_id_type=pl.DeviceIdType.MESH,
             )
 
-        rows = pl.ds(1, width)
+        groups = [pl.ds(1, width)] if width < 4 else [pl.ds(2, 2), pl.ds(1, 1), pl.ds(4, 1)]
+        rows = groups[0]
         first, last = pl.ds(0, ROWS), pl.ds(third, ROWS)
         result = [
             copy(0, relaxed.at[turn, pl.ds(0, 5), width], relaxed.at[turn, pl.ds(0, 5), 0], (right, me_y)),
@@ -160,6 +163,11 @@
             result.append(
                 copy(6 + way, sent.at[turn, way, 1, last], came.at[turn, way, width + 1, last], (left, beyond))
             )
+        for no, group in enumerate(groups[1:]):
+            for way, beyond in ((0, above), (1, below)):
+                result.append(
+                    copy(8 + 2 * no + way, sent.at[turn, way, group], came.at[turn, way, group], (me_x, beyond))
+                )
         return result
 
     def keep(self, turn, x, tile, values):
@@ -302,6 +310,19 @@
     solid_load = pltpu.make_async_copy(solid_in, solid_own, own_sem.at[4])
     medium_load = pltpu.make_async_copy(medium_in, medium_own, own_sem.at[5])
     coarse_load = pltpu.make_async_copy(coarse_in, coarse_own, own_sem.at[6])
+    barrier = pltpu.get_barrier_semaphore()
+    for device in (
+        (left, below),
+        (left, above),
+        (right, below),
+        (right, above),
+        (left, me_y),
+        (right, me_y),
+        (me_x, below),
+        (me_x, above),
+    ):
+        pl.semaphore_signal(barrier, inc=1, device_id=device, device_id_type=pl.DeviceIdType.MESH)
+
     medium_load.start()
     for x in (0, 3):
         plane_load(x).start()
@@ -310,19 +331,6 @@
         plane_load(x).start()
     coarse_load.start()
 
-    barrier = pltpu.get_barrier_semaphore()
-    for device in (
-        (left, me_y),
-        (right, me_y),
-        (me_x, below),
-        (me_x, above),
-        (left, below),
-        (left, above),
-        (right, below),
-        (right, above),
-    ):
-        pl.semaphore_signal(barrier, inc=1, device_id=device, device_id_type=pl.DeviceIdType.MESH)
-
     shear = jnp.broadcast_to(shear_ref[...], (ROWS, LANES))
     excess = 1.0 / shear - 0.5
     rates = [1.0 / (2.0**t * excess + 0.5) for t in range(3)]
@@ -381,22 +389,22 @@
             edges(turn, x)
 
         if turn > 0:
-            receive(fine, turn - 1, ROWS_ONLY + FROM_LEFT)
+            receive(fine, turn - 1, ROWS_0 + ROWS_3 + ROWS_ONLY + FROM_LEFT)
         plane(0)
-        if turn == 0:
-            pl.semaphore_wait(barrier, 8)
-        send(fine, turn, FROM_RIGHT)
         if turn > 0:
+            send(fine, turn, FROM_RIGHT + ROWS_0)
             receive(fine, turn - 1, FROM_RIGHT)
         plane(3)
-        send(fine, turn, FROM_LEFT)
+        if turn > 0:
+            send(fine, turn, FROM_LEFT + ROWS_3)
 
         def inner(x, carry):
             plane(x)
             return carry
 
         lax.fori_loop(1, 3, inner, 0)
-        send(fine, turn, ROWS_ONLY)
+        if turn > 0:
+            send(fine, turn, ROWS_ONLY)
 
     medium_load.wait()
     sweep(medium, lambda x, tile: medium.keep(0, x, tile, collide(taken(medium_own, x, tile), rates[1], None)))
@@ -413,6 +421,8 @@
             fine.keep(0, x, tile, collide(taken(fine_own, x, tile), rates[2], solid_tile(solid_own, x, tile)))
 
     fine_pass(0, first)
+    pl.semaphore_wait(barrier, 8)
+    send(fine, 0, CORNERS_FIRST + ROWS_0 + ROWS_3)
     coarse_load.wait()
     sweep(coarse, lambda x, tile: coarse.keep(0, x, tile, collide(taken(coarse_own, x, tile), rates[0], None)))
 
@@ -469,7 +479,7 @@
     for turn in range(SUBSTEPS - 1):
         sent_off(fine, turn)
 
-    receive(fine, SUBSTEPS - 1, ROWS_ONLY)
+    receive(fine, SUBSTEPS - 1, ROWS_0 + ROWS_3 + ROWS_ONLY)
 
     def inner(x, carry):
         for tile in range(fine.tiles):
@@ -522,7 +532,7 @@
         relaxed = pltpu.VMEM((turns, 19, width + 2, tiles, ROWS, LANES), jnp.float32)
         edge_rows = pltpu.VMEM((turns, 2, width + 2, lines, LANES), jnp.float32)
         scratch += [edge_rows] if t == 2 else [relaxed, edge_rows, edge_rows]
-        scratch += [pltpu.SemaphoreType.DMA((turns, 8))] * 2
+        scratch += [pltpu.SemaphoreType.DMA((turns, 12 if t == 2 else 8))] * 2
     given = (coarse_pops, medium_pops, fine_pops, solid_cells)
     in_vmem = pl.BlockSpec(memory_space=pltpu.VMEM)
     held = pl.pallas_call(

time: 45.4 us -> 45.4 us (level)
  no operation moved by 1% of the time
where the time goes in v3:
time: 45.4 us; the launch traced here: 45.2 us
  Pallas kernels  44 us (97%)
  between operations  1.29 us (3%)
    pallas_call x1, Pallas kernels, shards(): pl.pallas_call(lambda *refs: kernel(sizes, *refs), out_shape=tuple((pltpu...  42.7 us
    pallas_call x1, Pallas kernels, shards(): pl.pallas_call(finish, out_shape=tuple((jax.ShapeDtypeStruct(pops.shape,...  1.21 us

profile of v3, /device:TPU:1, one launch (start us, length us, event | category | flops | bytes accessed | tf_op | source)
XLA Modules:
  0.0 45.2 jit_solution(4164454448081470139)
XLA Ops:
  1.3 42.7 %shard_map.76 = (f32[19,1,8,128]{3,2,1,0:T(8,128)S(1)}, f32[19,2,8,256]{3,2,1,0:T(8,128)S(1)}, f32[19,4,8,512]{3,2,1,0:T(8,128)S(1)}, s32[4,8,512]{2,1,0:T(8,128...) custom-call(f32[19,1,8,128]{3,2,1,0:T(8,128)} %refs_0_.1, f32[19,2,8,256]{3,2,1,0:T(8,128)} %refs_1_.1, ...), custom_call_target="tpu_custom_call" | custom-call | tf_op jit(solution)/shard_map/pallas_call | solution.py:538
  44.0 1.2 %shard_map.77 = (f32[19,1,8,128]{3,2,1,0:T(8,128)}, f32[19,2,8,256]{3,2,1,0:T(8,128)}, f32[19,4,8,512]{3,2,1,0:T(8,128)}) custom-call(f32[19,1,8,128]{3,2,1,0:T(8,128)S(1)} %get-tuple-element.8.coarse, f32[19,2,8,256]{3,2,1,0:T(8,128)S(1)} %get-tuple-element.9.medium, f32[19,4,8,512]{3,2,1,0:T(8,128)S(1)} %get-tuple-element.10.inner, ...), custom_call_target="tpu_custom_call" | custom-call | tf_op jit(solution)/shard_map/pallas_call | solution.py:548
